TPU v7x, 32 devices: a whole 2x2x4 slice. The times are simulated.
32 devices in a mesh: groups: 2 (over y), expert: 4 (over z), width: 4 (over x, core).
Axes of the slice: x: 2, y: 2, z: 4, core: 2. Of those that a mesh axis runs over, the one named last changes fastest.
Arguments:
- residuals: bfloat16 [8192, 8192], P(('groups', 'expert'), 'width'), parts along dimension 0, may hold values from -6 to 6
- routes: int32 [8192, 1], P(('groups', 'expert')), parts along dimension 0, may hold values from 0 to 3; in each aligned block of 1024 rows (0 to 1023, 1024 to 2047, ...) at most 512 rows name the same one
- router_gate: bfloat16 [8192], P(('groups', 'expert')), parts along dimension 0, may hold values from 0.5 to 1
- enc_weight: bfloat16 [8, 8192, 256], P(('groups', 'expert'), 'width'), parts along dimension 0, may hold values from -0.0625 to 0.0625
- dec_weight: bfloat16 [8, 256, 8192], P(('groups', 'expert'), None, 'width'), parts along dimension 0, may hold values from -0.375 to 0.375
- enc_first: float32 [8, 8192, 256], P(('groups', 'expert'), 'width'), parts along dimension 0, may hold values from -3 to 3
- enc_second: float32 [8, 8192, 256], P(('groups', 'expert'), 'width'), parts along dimension 0, may hold values from 0.05 to 1
- dec_first: float32 [8, 256, 8192], P(('groups', 'expert'), None, 'width'), parts along dimension 0, may hold values from -3 to 3
- dec_second: float32 [8, 256, 8192], P(('groups', 'expert'), None, 'width'), parts along dimension 0, may hold values from 0.05 to 1
Outputs:
- new_enc_first: float32 [8, 8192, 256], P(('groups', 'expert'), 'width'), parts along dimension 0
- new_enc_second: float32 [8, 8192, 256], P(('groups', 'expert'), 'width'), parts along dimension 0
- enc_update: bfloat16 [8, 8192, 256], P(('groups', 'expert'), 'width'), parts along dimension 0
- new_dec_first: float32 [8, 256, 8192], P(('groups', 'expert'), None, 'width'), parts along dimension 0
- new_dec_second: float32 [8, 256, 8192], P(('groups', 'expert'), None, 'width'), parts along dimension 0
- dec_update: bfloat16 [8, 256, 8192], P(('groups', 'expert'), None, 'width'), parts along dimension 0
There are 2 independent parts, one for each index of `groups`. A program takes and returns all parts, laid end to end along the dimension named above; each array names one. Nothing has to cross between parts.
Inputs may be any that keep to these rules, and one draw needn't show every extreme that they name: `routes`: each row names one expert. In each aligned block of 1024 rows no expert is named by more than 512 rows, a bound that some block reaches.
All inputs are finite; a program needn't handle non-finite values.
Results may differ from a plain program's by a relative error of at most 0.0039.
Values may be sent and summed in bfloat16 or wider, within the bound.
A program may use at most 128 MiB of HBM per device.

v0:
```python
import math

import jax
import jax.numpy as jnp
from jax import lax
from jax.sharding import PartitionSpec as P

STEP = 100


L1_COEF = 1.0
CLIP_RATIO = 0.5
BETA_ONE = 0.9
BETA_TWO = 0.999
ADAM_EPS = 1e-08
FIRST_DIMS = (((0,), (0,)), ((), ()))
LAST_DIMS = (((1,), (1,)), ((), ()))


def adam_step(first, second, gradient, factor):
    scaled = factor * gradient
    new_first = BETA_ONE * first + (1.0 - BETA_ONE) * scaled
    new_second = BETA_TWO * second + (1.0 - BETA_TWO) * scaled * scaled
    corrected = new_first / (1.0 - BETA_ONE**STEP)
    spread = jnp.sqrt(new_second / (1.0 - BETA_TWO**STEP))
    return (new_first, new_second, (corrected / (spread + ADAM_EPS)).astype(jnp.bfloat16))


def body(
    residuals,
    routes,
    router_gate,
    enc_weight,
    dec_weight,
    enc_first,
    enc_second,
    dec_first,
    dec_second,
):
    expert_count = lax.axis_size("expert")
    width_count = lax.axis_size("width")
    local_rows = residuals.shape[0]
    feature_cols = residuals.shape[1]
    slot_cap = 2 * local_rows // expert_count
    slots = slot_cap * expert_count
    expert_ids = jnp.arange(expert_count, dtype=jnp.int32)
    onehot = (routes == expert_ids[None, :]).astype(jnp.int32)
    within = jnp.sum(jnp.cumsum(onehot, axis=0) * onehot, axis=1) - 1
    target = routes[:, 0] * slot_cap + within
    send_rows = jnp.zeros((slots, feature_cols), jnp.bfloat16).at[target].set(residuals)
    send_gate = jnp.zeros((slots,), jnp.bfloat16).at[target].set(router_gate)
    bucket_rows = send_rows.reshape(expert_count, slot_cap, feature_cols)
    bucket_gate = send_gate.reshape(expert_count, slot_cap)
    w_enc = enc_weight[0]
    w_dec = dec_weight[0]
    got_rows, got_gate = (
        lax.all_to_all(bucket_rows, "expert", split_axis=0, concat_axis=0, tiled=True),
        lax.all_to_all(bucket_gate, "expert", split_axis=0, concat_axis=0, tiled=True),
    )
    slot_rows = got_rows.reshape(slots, feature_cols)
    slot_gate = got_gate.reshape(slots).astype(jnp.float32)
    partial_pre = jnp.dot(slot_rows, w_enc, preferred_element_type=jnp.float32)
    preact = lax.psum(partial_pre, "width")
    codes = jnp.maximum(preact, 0.0).astype(jnp.bfloat16)
    decoded = jnp.dot(codes, w_dec, preferred_element_type=jnp.float32)
    errors = slot_gate[:, None] * decoded - slot_rows.astype(jnp.float32)
    grad_out = (2.0 * slot_gate[:, None] * errors).astype(jnp.bfloat16)
    grad_dec = lax.dot_general(codes, grad_out, FIRST_DIMS, preferred_element_type=jnp.float32)
    grad_codes = lax.psum(
        lax.dot_general(grad_out, w_dec, LAST_DIMS, preferred_element_type=jnp.float32).astype(
            jnp.bfloat16
        ),
        "width",
    ).astype(jnp.float32)
    grad_pre = jnp.where(codes > 0, grad_codes + L1_COEF, 0.0).astype(jnp.bfloat16)
    grad_enc = lax.dot_general(slot_rows, grad_pre, FIRST_DIMS, preferred_element_type=jnp.float32)
    local_square = jnp.sum(grad_enc * grad_enc) + jnp.sum(grad_dec * grad_dec)
    total = lax.psum(local_square, ("expert", "width"))
    param_count = (
        2.0 * expert_count * enc_weight.shape[0] * feature_cols * width_count * w_enc.shape[1]
    )
    factor = jnp.minimum(1.0, CLIP_RATIO * math.sqrt(param_count) / (jnp.sqrt(total) + 1e-06))
    enc_new_first, enc_new_second, enc_direction = adam_step(
        enc_first, enc_second, grad_enc[None], factor
    )
    dec_new_first, dec_new_second, dec_direction = adam_step(
        dec_first, dec_second, grad_dec[None], factor
    )
    return (
        enc_new_first,
        enc_new_second,
        enc_direction,
        dec_new_first,
        dec_new_second,
        dec_direction,
    )


def solution(mesh):
    in_specs = (
        P(("groups", "expert"), "width"),
        P(("groups", "expert"), None),
        P(("groups", "expert")),
        P(("groups", "expert"), "width", None),
        P(("groups", "expert"), None, "width"),
        P(("groups", "expert"), "width", None),
        P(("groups", "expert"), "width", None),
        P(("groups", "expert"), None, "width"),
        P(("groups", "expert"), None, "width"),
    )
    out_specs = (
        P(("groups", "expert"), "width", None),
        P(("groups", "expert"), "width", None),
        P(("groups", "expert"), "width", None),
        P(("groups", "expert"), None, "width"),
        P(("groups", "expert"), None, "width"),
        P(("groups", "expert"), None, "width"),
    )
    return jax.shard_map(body, mesh=mesh, in_specs=in_specs, out_specs=out_specs, check_vma=False)
```

profile of v0, /device:TPU:0, one launch (start us, length us, event | category | flops | bytes accessed | tf_op | source)
XLA Modules:
  0.0 384.1 jit_solution(13875583299192531444)
XLA Ops:
  7.2 0.0 copy-start
  7.2 0.8 fusion.16
  8.0 1.1 reduce-window.6
  9.1 0.2 slice_reduce_fusion
  9.3 0.2 reduce-window.9
  9.5 0.1 add_bitcast_fusion
  9.6 0.7 fusion.15
  10.3 0.7 compare_select_fusion
  11.0 7.8 %scatter_custom_fusion.1 = bf16[2048]{0:T(1024)(128)(2,1)S(1)} fusion(s32[1024]{0:T(1024)S(1)} %bitcast.59, bf16[1024]{0:T(1024)(128)(2,1)} %param.11, bf16[]{:T(256)} %constant.19.clone.1), kind=kCustom, calls=%fused_computation.38 | custom fusion | bytes 4608 | tf_op jit(solution)/shard_map/scatter | solution.py:51
  18.8 0.5 broadcast.61
  19.3 0.7 reduce.2
  20.0 0.6 reshape.95
  20.6 6.3 %all-to-all-start.1 = ((bf16[4,2,256]{2,1,0:T(2,128)(2,1)}), bf16[4,2,256]{2,1,0:T(2,128)(2,1)S(1)}, u32[]{:S(2)}, u32[]{:S(2)}) async-start(bf16[4,2,256]{2,1,0:T(2,128)(2,1)} %reshape.95), calls=%async_computation.1 | async-start | bytes 8192 | tf_op jit(solution)/shard_map/all_to_all | solution.py:58
  26.9 12.3 %scatter_custom_fusion = bf16[2048,2048]{1,0:T(8,128)(2,1)} fusion(s32[1024]{0:T(1024)S(1)} %bitcast.60, bf16[1024,2048]{1,0:T(8,128)(2,1)} %param.9, bf16[]{:T(256)} %constant.19.clone.1), kind=kCustom, calls=%fused_computation.3 | custom fusion | bytes 8389120 | tf_op jit(solution)/shard_map/scatter | solution.py:50
  39.1 0.0 all-to-all-done.1
  39.1 0.0 copy-start.5
  39.1 5.8 %all-to-all-start = ((bf16[4,512,2048]{2,1,0:T(8,128)(2,1)}), bf16[4,512,2048]{2,1,0:T(8,128)(2,1)}, u32[]{:S(2)}, u32[]{:S(2)}) async-start(bf16[4,512,2048]{2,1,0:T(8,128)(2,1)} %bitcast.52), calls=%async_computation | async-start | bytes 16777216 | tf_op jit(solution)/shard_map/all_to_all | solution.py:57
  44.9 0.2 all-reduce.3.cloned.1.call-start
  45.2 182.8 %all-to-all-done = bf16[4,512,2048]{2,1,0:T(8,128)(2,1)} async-done(((bf16[4,512,2048]{2,1,0:T(8,128)(2,1)}), bf16[4,512,2048]{2,1,0:T(8,128)(2,1)}, u32[]{:S(2)}, u32[]{:S(2)}) %all-to-all-start) | async-done | bytes 8388640 | tf_op jit(solution)/shard_map/all_to_all | solution.py:57
  228.0 0.0 copy-done.5
  228.0 7.1 %fusion.9 = f32[2048,256]{1,0:T(8,128)} fusion(bf16[2048,2048]{1,0:T(8,128)(2,1)} %bitcast.6, bf16[1,2048,256]{2,1,0:T(8,128)(2,1)S(1)} %copy-done.5), kind=kOutput, calls=%fused_computation.23 | convolution fusion | flops 2147483648 | bytes 11534336 | tf_op jit(solution)/shard_map/dot_general | solution.py:62
  235.1 40.8 %all-reduce.4 = bf16[2048,256]{1,0:T(8,128)(2,1)S(1)} all-reduce(f32[2048,256]{1,0:T(8,128)} %fusion.9), channel_id=1, replica_groups=mesh['groups'=2,'expert'=4,'width'=4] {'width'}, use_global_device_ids=true, to_apply=%region_4.5 | all-reduce | flops 524288 | bytes 3145728 | tf_op jit(solution)/shard_map/psum | solution.py:63
  275.9 0.0 copy-done
  275.9 0.0 copy-start.2
  275.9 5.7 %multiply_convert_fusion = bf16[2048,2048]{1,0:T(8,128)(2,1)S(1)} fusion(bf16[2048,2048]{1,0:T(8,128)(2,1)} %bitcast.6, f32[2048]{0:T(1024)S(1)} %bitcast.56, f32[2048]{0:T(1024)S(1)} %broadcast_multiply_fusion, bf16[1,256,2048]{2,1,0:T(8,128)(2,1)S(1)} %copy-done, bf16[2048,256]{1,0:T(8,128)(2,1)S(1)} %all-reduce.4), kind=kOutput, calls=%fused_computation.2 | convolution fusion | flops 2170028032 | bytes 18890752 | tf_op jit(solution)/shard_map/dot_general | solution.py:65
  281.6 0.0 copy-done.2
  281.6 0.0 copy-start.1
  281.6 3.2 copy-done.1
  284.8 3.4 convolution_convert_fusion
  288.1 0.0 all-reduce.3.cloned.1.call-update
  288.2 6.9 %multiply_reduce_fusion = (f32[]{:T(128)}, f32[256,2048]{1,0:T(8,128)S(1)}) fusion(bf16[2048,2048]{1,0:T(8,128)(2,1)} %copy-done.1, bf16[2048,256]{1,0:T(8,128)(2,1)} %copy-done.2), kind=kOutput, calls=%fused_computation.16 | convolution fusion | flops 2150105088 | bytes 11534340 | tf_op jit(solution)/shard_map/dot_general | solution.py:68
  295.1 28.9 %all-reduce.3.cloned.1.call-done = bf16[2048,256]{1,0:T(8,128)(2,1)} async-done(((bf16[2048,256]{1,0:T(8,128)(2,1)}), bf16[2048,256]{1,0:T(8,128)(2,1)}) %all-reduce.3.cloned.1.call-update) | async-done | bytes 1048592 | tf_op jit(solution)/shard_map/psum | solution.py:69
  324.0 8.4 %multiply_reduce_fusion.1 = (f32[]{:T(128)}, f32[2048,256]{1,0:T(8,128)}) fusion(bf16[2048,2048]{1,0:T(8,128)(2,1)} %bitcast.6, bf16[2048,256]{1,0:T(8,128)(2,1)} %all-reduce.3.cloned.1.call-done, bf16[2048,256]{1,0:T(8,128)(2,1)} %copy-done.2), kind=kOutput, calls=%fused_computation.17 | convolution fusion | flops 2152726528 | bytes 12582916 | tf_op jit(solution)/shard_map/dot_general | solution.py:76
  333.7 33.2 %psum.23 = f32[]{:T(128)} all-reduce(f32[]{:T(128)S(6)} %add.64), channel_id=1, replica_groups=mesh['groups'=2,'expert'=4,'width'=4] {'expert','width'}, use_global_device_ids=true, to_apply=%region_9.10 | all-reduce | flops 1 | bytes 8 | tf_op jit(solution)/shard_map/psum | solution.py:78
  367.7 0.0 copy-start.3
  367.7 0.0 copy-start.4
  367.7 6.3 %divide_convert_fusion.1 = (bf16[1,2048,256]{2,1,0:T(8,128)(2,1)}, f32[1,2048,256]{2,1,0:T(8,128)}, f32[1,2048,256]{2,1,0:T(8,128)}) fusion(f32[2048,256]{1,0:T(8,128)} %get-tuple-element.13, f32[]{:T(128)S(6)} %min.3, f32[1,2048,256]{2,1,0:T(8,128)} %param.15, f32[1,2048,256]{2,1,0:T(8,128)} %param.14), kind=kLoop, calls=%fused_computation.15 | loop fusion | flops 6815744 | bytes 11534340 | tf_op jit(solution)/shard_map/convert_element_type | solution.py:26
  374.0 0.0 copy-done.3
  374.0 0.0 copy-done.4
  374.0 3.3 divide_convert_fusion
  (5 shorter events, 0.0 us)
Async XLA Ops:
  7.2 268.7 %copy-start = (bf16[1,256,2048]{2,1,0:T(8,128)(2,1)S(1)}, bf16[1,256,2048]{2,1,0:T(8,128)(2,1)}, u32[]{:S(2)}) copy-start(bf16[1,256,2048]{2,1,0:T(8,128)(2,1)} %param.13) | copy-start | bytes 3145732
  20.6 18.6 %all-to-all-start.1 = ((bf16[4,2,256]{2,1,0:T(2,128)(2,1)}), bf16[4,2,256]{2,1,0:T(2,128)(2,1)S(1)}, u32[]{:S(2)}, u32[]{:S(2)}) async-start(bf16[4,2,256]{2,1,0:T(2,128)(2,1)} %reshape.95), calls=%async_computation.1 | async-start | bytes 8192 | tf_op jit(solution)/shard_map/all_to_all | solution.py:58
  39.1 188.9 %copy-start.5 = (bf16[1,2048,256]{2,1,0:T(8,128)(2,1)S(1)}, bf16[1,2048,256]{2,1,0:T(8,128)(2,1)}, u32[]{:S(2)}) copy-start(bf16[1,2048,256]{2,1,0:T(8,128)(2,1)} %param.12) | copy-start | bytes 3145732
  39.1 188.9 %all-to-all-start = ((bf16[4,512,2048]{2,1,0:T(8,128)(2,1)}), bf16[4,512,2048]{2,1,0:T(8,128)(2,1)}, u32[]{:S(2)}, u32[]{:S(2)}) async-start(bf16[4,512,2048]{2,1,0:T(8,128)(2,1)} %bitcast.52), calls=%async_computation | async-start | bytes 16777216 | tf_op jit(solution)/shard_map/all_to_all | solution.py:57
  44.9 279.1 %all-reduce.3.cloned.1.call-start = ((), (), s32[]{:S(2)}) async-start(), calls=%async_computation.2 | async-start | bytes 2097152 | tf_op jit(solution)/shard_map/psum | solution.py:69
  275.9 5.7 %copy-start.2 = (bf16[2048,256]{1,0:T(8,128)(2,1)}, bf16[2048,256]{1,0:T(8,128)(2,1)S(1)}, u32[]{:S(2)}) copy-start(bf16[2048,256]{1,0:T(8,128)(2,1)S(1)} %all-reduce.4) | copy-start | bytes 3145732
  281.6 3.2 copy-start.1
  367.7 6.3 %copy-start.3 = (f32[1,256,2048]{2,1,0:T(8,128)S(1)}, f32[1,256,2048]{2,1,0:T(8,128)}, u32[]{:S(2)}) copy-start(f32[1,256,2048]{2,1,0:T(8,128)} %param.17) | copy-start | bytes 6291460
  367.7 6.3 %copy-start.4 = (f32[1,256,2048]{2,1,0:T(8,128)S(1)}, f32[1,256,2048]{2,1,0:T(8,128)}, u32[]{:S(2)}) copy-start(f32[1,256,2048]{2,1,0:T(8,128)} %param.16) | copy-start | bytes 6291460
Sparse Core Ops, SparseCore 0:
  288.3 35.7 all-reduce.2
where the time goes:
time: 385 us; the launch traced here: 384 us
  waiting for transfers between devices  212 us (55%)
  blocking collectives  74 us (19%)
  matrix products  31.4 us (8%)
  local copies, waits for them, and re-layouts  24.6 us (6%)
  between operations  16.2 us (4%)
  other arithmetic  13.8 us (4%)
  starting transfers between devices  12.3 us (3%)
    all_to_all x1, waiting for transfers between devices, body(): lax.all_to_all(bucket_rows, 'expert', split_axis=0, concat_axis=0, tiled=...  183 us
    psum x1, blocking collectives, body(): preact = lax.psum(partial_pre, 'width')  40.8 us
    psum x1, blocking collectives, body(): total = lax.psum(local_square, ('expert', 'width'))  33.2 us
    psum x1, waiting for transfers between devices, body(): lax.psum(lax.dot_general(grad_out, w_dec, LAST_DIMS, preferred_element_ty...  28.9 us
    scatter x1, local copies, waits for them, and re-layouts, body(): jnp.zeros((slots, feature_cols), jnp.bfloat16).at[target].set(residuals)  12.3 us
    convert_element_type x2, other arithmetic, adam_step(): (corrected / (spread + ADAM_EPS)).astype(jnp.bfloat16)  9.54 us
    dot_general x1, matrix products, body(): lax.dot_general(slot_rows, grad_pre, FIRST_DIMS, preferred_element_type=j...  8.4 us
    scatter x1, local copies, waits for them, and re-layouts, body(): send_gate = jnp.zeros((slots,), jnp.bfloat16).at[target].set(router_gate)  7.75 us
  transfers between devices with their start and end apart: 3, of which 2 were waited for; matrix products, arithmetic and copies ran while one was open for 5% of the time, Pallas kernels for 0%

commit v1 on v0

v1 whole, which is shorter than its diff:
```python
import functools
import math

import jax
import jax.numpy as jnp
from jax import lax
from jax.experimental import pallas as pl
from jax.experimental.pallas import tpu as pltpu
from jax.sharding import PartitionSpec as P

STEP = 100
L1_COEF = 1.0
CLIP_RATIO = 0.5
BETA_ONE = 0.9
BETA_TWO = 0.999
ADAM_EPS = 1e-08
MESH = pl.DeviceIdType.MESH
BF, F32 = jnp.bfloat16, jnp.float32


def dot(a, b, ca=1, cb=0):
    return lax.dot_general(a, b, (((ca,), (cb,)), ((), ())), preferred_element_type=F32)


def adam_step(first, second, gradient, factor):
    scaled = factor * gradient
    new_first = BETA_ONE * first + (1.0 - BETA_ONE) * scaled
    new_second = BETA_TWO * second + (1.0 - BETA_TWO) * scaled * scaled
    corrected = new_first / (1.0 - BETA_ONE**STEP)
    spread = jnp.sqrt(new_second / (1.0 - BETA_TWO**STEP))
    return (new_first, new_second, (corrected / (spread + ADAM_EPS)).astype(BF))


def kernel(
    experts, widths, cap, chunk, tile,
    x_ref, route_ref, gate_ref, we_ref, wd_ref,
    ge_ref, gd_ref, tot_ref,
    snd, rows, gsnd, grow, pre, pre_in, codes, gc, gc_in, gp, acc, gout, norm,
    z_send, z_recv, g_send, g_recv, p_send, p_recv, c_send, c_recv,
    b_send, b_recv, q_send, q_recv, n_send, n_recv,
):
    local_rows, feats = x_ref.shape
    halves = cap // chunk
    count = experts * halves
    quarter = chunk // widths
    me = lax.axis_index("expert")
    mw = lax.axis_index("width")

    def zdev(d):
        return {"expert": lax.rem(me + d, experts)}

    def wdev(w):
        return {"width": lax.rem(mw + w, widths)}

    barrier = pltpu.get_barrier_semaphore()
    for d in range(1, experts):
        pl.semaphore_signal(barrier, inc=1, device_id=zdev(d), device_id_type=MESH)
    for w in range(1, widths):
        pl.semaphore_signal(barrier, inc=1, device_id=wdev(w), device_id_type=MESH)

    pad = max(16, experts)
    route = route_ref[...]
    named = (lax.broadcasted_iota(jnp.int32, (pad, local_rows), 0) == route).astype(BF)
    upper = (
        lax.broadcasted_iota(jnp.int32, (local_rows, local_rows), 0)
        <= lax.broadcasted_iota(jnp.int32, (local_rows, local_rows), 1)
    ).astype(BF)
    within = jnp.sum(dot(named, upper) * named.astype(F32), axis=0, keepdims=True)
    target = route * cap + within.astype(jnp.int32) - 1
    pl.semaphore_wait(barrier, experts + widths - 2)

    half_way = experts // 2
    order = [0] + sorted(range(1, experts), key=lambda d: (abs(d - half_way), d))

    def z_copy(n, d):
        m = n - halves
        return pltpu.make_async_remote_copy(
            snd.at[m], rows.at[n], z_send.at[m], z_recv.at[m], device_id=zdev(d), device_id_type=MESH
        )

    def g_copy(n, d):
        m = n - halves
        return pltpu.make_async_remote_copy(
            gsnd.at[m], grow.at[n], g_send.at[m], g_recv.at[m], device_id=zdev(d), device_id_type=MESH
        )

    for j in [*range(1, experts), 0]:
        expert = lax.rem(me + order[j], experts)
        for h in range(halves):
            n = j * halves + h
            base = expert * cap + h * chunk
            slot = lax.broadcasted_iota(jnp.int32, (chunk, local_rows), 0) + base
            pick = (slot == target).astype(BF)
            to, gto = (snd.at[n - halves], gsnd.at[n - halves]) if j else (rows.at[n], grow.at[n])
            gto[...] = dot(gate_ref[...], pick, 1, 1).astype(BF)

            @pl.loop(0, feats // tile)
            def _(f):
                cols = pl.ds(pl.multiple_of(f * tile, tile), tile)
                to[:, cols] = dot(pick, x_ref[:, cols]).astype(BF)

            if j:
                g_copy(n, order[j]).start()
                z_copy(n, order[j]).start()

    ge_ref[...] = jnp.zeros_like(ge_ref)
    gd_ref[...] = jnp.zeros_like(gd_ref)
    mine = pl.ds(pl.multiple_of(mw * quarter, quarter), quarter)

    def scatter(n, w, src, dst, ssem, rsem):
        theirs = lax.rem(mw + w, widths)
        return pltpu.make_async_remote_copy(
            src.at[n, pl.ds(pl.multiple_of(theirs * quarter, quarter), quarter)],
            dst.at[n, w - 1],
            ssem.at[n, w - 1], rsem.at[n, w - 1], device_id=wdev(w), device_id_type=MESH,
        )

    def gather(n, w, buf, ssem, rsem):
        return pltpu.make_async_remote_copy(
            buf.at[n, mine], buf.at[n, mine],
            ssem.at[n, w - 1], rsem.at[n, w - 1], device_id=wdev(w), device_id_type=MESH,
        )

    def gather_wait(n, w, buf, ssem, rsem):
        src = lax.rem(mw + widths - w, widths)
        theirs = pl.ds(pl.multiple_of(src * quarter, quarter), quarter)
        pltpu.make_async_remote_copy(
            buf.at[n, theirs], buf.at[n, theirs],
            ssem.at[n, w - 1], rsem.at[n, w - 1], device_id=wdev(w), device_id_type=MESH,
        ).wait_recv()

    peers = range(1, widths)

    def stage_pre(n):
        @pl.when(n >= halves)
        def _():
            z_copy(n, 1).wait_recv()
            g_copy(n, 1).wait_recv()

        pre[n] = dot(rows[n], we_ref[...])
        for w in peers:
            scatter(n, w, pre, pre_in, p_send, p_recv).start()

    def stage_codes(n):
        total = pre[n, mine]
        for w in peers:
            scatter(n, w, pre, pre_in, p_send, p_recv).wait_recv()
            total = total + pre_in[n, w - 1]
        codes[n, mine] = jnp.maximum(total, 0.0).astype(BF)
        for w in peers:
            gather(n, w, codes, c_send, c_recv).start()

    def stage_decode(n):
        for w in peers:
            gather_wait(n, w, codes, c_send, c_recv)
        gate = grow[n].astype(F32).T[:, :1]
        code = codes[n]
        acc[...] = jnp.zeros_like(acc)

        @pl.loop(0, feats // tile)
        def _(f):
            cols = pl.ds(pl.multiple_of(f * tile, tile), tile)
            w_dec = wd_ref[:, cols]
            errors = gate * dot(code, w_dec) - rows[n, :, cols].astype(F32)
            gout[:, cols] = (2.0 * gate * errors).astype(BF)
            go = gout[:, cols]
            acc[...] += dot(go, w_dec, 1, 1)
            gd_ref[:, cols] += dot(code, go, 0, 0)

        gc[n] = acc[...].astype(BF)
        for w in peers:
            scatter(n, w, gc, gc_in, b_send, b_recv).start()

    def stage_gradpre(n):
        total = gc[n, mine].astype(F32)
        for w in peers:
            scatter(n, w, gc, gc_in, b_send, b_recv).wait_recv()
            total = total + gc_in[n, w - 1].astype(F32)
        gp[n, mine] = jnp.where(codes[n, mine].astype(F32) > 0, total + L1_COEF, 0.0).astype(BF)
        for w in peers:
            gather(n, w, gp, q_send, q_recv).start()

    def stage_encgrad(n):
        for w in peers:
            gather_wait(n, w, gp, q_send, q_recv)
        grad_pre = gp[n]

        @pl.loop(0, feats // tile)
        def _(f):
            cols = pl.ds(pl.multiple_of(f * tile, tile), tile)
            ge_ref[cols, :] += dot(rows[n, :, cols], grad_pre, 0, 0)

    stages = (stage_pre, stage_codes, stage_decode, stage_gradpre, stage_encgrad)

    @pl.loop(0, count + len(stages) - 1)
    def _(t):
        for lag in reversed(range(len(stages))):
            @pl.when((t >= lag) & (t < count + lag))
            def _(lag=lag):
                stages[lag](t - lag)

    square = jnp.sum(ge_ref[...] * ge_ref[...]) + jnp.sum(gd_ref[...] * gd_ref[...])
    norm[0] = jnp.full(norm.shape[1:], square, F32)
    first = [
        pltpu.make_async_remote_copy(
            norm.at[0], norm.at[1 + w], n_send.at[w], n_recv.at[w], device_id=wdev(w), device_id_type=MESH
        )
        for w in peers
    ]
    for c in first:
        c.start()
    for c in first:
        c.wait()
    part = norm[0]
    for w in peers:
        part = part + norm[1 + w]
    norm[1] = part
    off = widths + 1
    second = [
        pltpu.make_async_remote_copy(
            norm.at[1], norm.at[off + d], n_send.at[widths + d], n_recv.at[widths + d],
            device_id=zdev(d), device_id_type=MESH,
        )
        for d in range(1, experts)
    ]
    for c in second:
        c.start()
    for c in second:
        c.wait()
    for d in range(1, experts):
        part = part + norm[off + d]
    tot_ref[...] = part

    @pl.loop(halves, count)
    def _(n):
        z_copy(n, 1).wait_send()
        g_copy(n, 1).wait_send()

    @pl.loop(0, count)
    def _(n):
        for w in peers:
            scatter(n, w, pre, pre_in, p_send, p_recv).wait_send()
            gather(n, w, codes, c_send, c_recv).wait_send()
            scatter(n, w, gc, gc_in, b_send, b_recv).wait_send()
            gather(n, w, gp, q_send, q_recv).wait_send()


def body(
    residuals, routes, router_gate, enc_weight, dec_weight, enc_first, enc_second, dec_first, dec_second
):
    experts = lax.axis_size("expert")
    widths = lax.axis_size("width")
    local_rows, feats = residuals.shape
    lat = enc_weight.shape[2]
    cap = 2 * local_rows // experts
    chunk = min(256, cap)
    tile = min(512, feats)
    halves = cap // chunk
    count = experts * halves
    quarter = chunk // widths
    far = count - halves
    route = routes.reshape(1, local_rows)
    gate = jnp.broadcast_to(router_gate[None, :], (16, local_rows))
    vmem = pl.BlockSpec(memory_space=pltpu.VMEM)
    dma = pltpu.SemaphoreType.DMA
    grad_enc, grad_dec, total = pl.pallas_call(
        functools.partial(kernel, experts, widths, cap, chunk, tile),
        out_shape=(
            jax.ShapeDtypeStruct((feats, lat), F32),
            jax.ShapeDtypeStruct((lat, feats), F32),
            jax.ShapeDtypeStruct((8, 128), F32),
        ),
        in_specs=[vmem] * 5,
        out_specs=(vmem,) * 3,
        scratch_shapes=[
            pltpu.VMEM((far, chunk, feats), BF),
            pltpu.VMEM((count, chunk, feats), BF),
            pltpu.VMEM((far, 16, chunk), BF),
            pltpu.VMEM((count, 16, chunk), BF),
            pltpu.VMEM((count, chunk, lat), F32),
            pltpu.VMEM((count, widths - 1, quarter, lat), F32),
            pltpu.VMEM((count, chunk, lat), BF),
            pltpu.VMEM((count, chunk, lat), BF),
            pltpu.VMEM((count, widths - 1, quarter, lat), BF),
            pltpu.VMEM((count, chunk, lat), BF),
            pltpu.VMEM((chunk, lat), F32),
            pltpu.VMEM((chunk, feats), BF),
            pltpu.VMEM((1 + widths + experts, 8, 128), F32),
            dma((far,)), dma((far,)), dma((far,)), dma((far,)),
            *[dma((count, widths - 1)) for _ in range(8)],
            dma((widths + experts,)), dma((widths + experts,)),
        ],
        compiler_params=pltpu.CompilerParams(
            collective_id=0, has_side_effects=True, vmem_limit_bytes=56 * 1024 * 1024
        ),
        cost_estimate=pl.CostEstimate(
            flops=10 * count * chunk * feats * lat, bytes_accessed=16 * feats * lat, transcendentals=0
        ),
    )(residuals, route, gate, enc_weight[0], dec_weight[0])
    param_count = 2.0 * experts * enc_weight.shape[0] * feats * widths * lat
    norm = jnp.sqrt(total[0, 0])
    factor = jnp.minimum(1.0, CLIP_RATIO * math.sqrt(param_count) / (norm + 1e-06))
    return (
        *adam_step(enc_first, enc_second, grad_enc[None], factor),
        *adam_step(dec_first, dec_second, grad_dec[None], factor),
    )


def solution(mesh):
    row = P(("groups", "expert"), "width")
    enc = P(("groups", "expert"), "width", None)
    dec = P(("groups", "expert"), None, "width")
    in_specs = (row, P(("groups", "expert"), None), P(("groups", "expert")), enc, dec, enc, enc, dec, dec)
    out_specs = (enc, enc, enc, dec, dec, dec)
    return jax.shard_map(body, mesh=mesh, in_specs=in_specs, out_specs=out_specs, check_vma=False)
```

time: 385 us -> 248 us (0.64)
  Pallas kernels: 0 us -> 235 us
  waiting for transfers between devices: 212 us -> 0 us
  blocking collectives: 74 us -> 0 us
  matrix products: 31.4 us -> 0 us
  local copies, waits for them, and re-layouts: 24.6 us -> 2.51 us
  between operations: 16.2 us -> 1.42 us
  starting transfers between devices: 12.3 us -> 0 us
  other arithmetic: 13.8 us -> 8.31 us
    pallas_call x0 -> x1, Pallas kernels: none -> 235 us  [body(): pl.pallas_call(functools.partial(kernel, experts, widths, cap, chunk, til...]
    all_to_all x2 -> x0, waiting for transfers between devices: 183 us -> none  [the longest x1 183 us: body(): lax.all_to_all(bucket_rows, 'expert', split_axis=0, concat_axis=0, tiled=...]
    psum x2 -> x0, blocking collectives: 74 us -> none  [the longest x1 40.8 us: body(): preact = lax.psum(partial_pre, 'width')]
    dot_general x5 -> x0, matrix products: 31.4 us -> none  [the longest x1 8.4 us: body(): lax.dot_general(slot_rows, grad_pre, FIRST_DIMS, preferred_element_type=j...]
    psum x1 -> x0, waiting for transfers between devices: 28.9 us -> none  [body(): lax.psum(lax.dot_general(grad_out, w_dec, LAST_DIMS, preferred_element_ty...]
    scatter x2 -> x0, local copies, waits for them, and re-layouts: 20 us -> none  [the longest x1 12.3 us: body(): jnp.zeros((slots, feature_cols), jnp.bfloat16).at[target].set(residuals)]
    all_to_all x2 -> x0, starting transfers between devices: 12.1 us -> none  [the longest x1 6.32 us: body(): lax.all_to_all(bucket_gate, 'expert', split_axis=0, concat_axis=0, tiled=...]
    convert_element_type x4 -> x2, other arithmetic: 10.3 us -> 8.31 us  [adam_step(): return (new_first, new_second, (corrected / (spread + ADAM_EPS)).astype(BF))]
  transfers between devices with their start and end apart: 3 -> 0, of which waited for: 2 -> 0; matrix products, arithmetic and copies ran while one was open for 5% -> 0% of each run, Pallas kernels for 0% -> 0%
where the time goes in v1:
time: 248 us
  Pallas kernels  235 us (95%)
  other arithmetic  8.31 us (3%)
  local copies, waits for them, and re-layouts  2.51 us (1%)
    pallas_call x1, Pallas kernels, body(): pl.pallas_call(functools.partial(kernel, experts, widths, cap, chunk, til...  235 us
    convert_element_type x2, other arithmetic, adam_step(): return (new_first, new_second, (corrected / (spread + ADAM_EPS)).astype(BF))  8.31 us

profile of v1, /device:TPU:0, one launch (start us, length us, event | category | flops | bytes accessed | tf_op | source)
XLA Modules:
  0.0 247.5 jit_solution(10597319768474844097)
XLA Ops:
  0.6 1.3 broadcast_in_dim.2.gate_ref
  1.9 0.0 copy-start
  1.9 0.0 copy-start.1
  1.9 235.3 %shard_map.136 = (f32[2048,256]{1,0:T(8,128)}, f32[256,2048]{1,0:T(8,128)}, f32[8,128]{1,0:T(8,128)}) custom-call(bf16[1024,2048]{1,0:T(8,128)(2,1)} %x_ref.1, s32[1,1024]{1,0:T(1,128)} %bitcast.22, bf16[16,1024]{1,0:T(8,128)(2,1)} %broadcast_in_dim.2.gate_ref, bf16[2048,256]{1,0:T(8,128)(2,1)} %bitcast.20, bf16[256,2048]{1,0:T(8,128)(2,1)} %bitcast.21), custom_call_target="tpu_custom_call" | custom-call | flops 10737418240 | bytes 8388608 | tf_op jit(solution)/shard_map/pallas_call | solution.py:266
  237.2 1.2 slice.3
  239.1 0.0 copy-done
  239.1 0.0 copy-done.1
  239.1 0.0 copy-start.2
  239.2 0.0 copy-start.3
  239.2 0.0 copy-start.4
  239.2 5.0 %divide_convert_fusion.1 = (bf16[1,2048,256]{2,1,0:T(8,128)(2,1)}, f32[1,2048,256]{2,1,0:T(8,128)}, f32[1,2048,256]{2,1,0:T(8,128)}) fusion(f32[2048,256]{1,0:T(8,128)} %get-tuple-element.10, f32[]{:T(128)} %bitcast.3, f32[1,2048,256]{2,1,0:T(8,128)S(1)} %copy-done, f32[1,2048,256]{2,1,0:T(8,128)S(1)} %copy-done.1), kind=kLoop, calls=%fused_computation.9 | loop fusion | flops 6815744 | bytes 11534340 | tf_op jit(solution)/shard_map/convert_element_type | solution.py:31
  244.2 0.0 copy-done.2
  244.2 0.0 copy-done.3
  244.2 0.0 copy-done.4
  244.2 3.3 %divide_convert_fusion = (bf16[1,256,2048]{2,1,0:T(8,128)(2,1)}, f32[1,256,2048]{2,1,0:T(8,128)}, f32[1,256,2048]{2,1,0:T(8,128)}) fusion(f32[256,2048]{1,0:T(8,128)S(1)} %copy-done.4, f32[]{:T(128)} %bitcast.3, f32[1,256,2048]{2,1,0:T(8,128)S(1)} %copy-done.2, f32[1,256,2048]{2,1,0:T(8,128)S(1)} %copy-done.3), kind=kLoop, calls=%fused_computation.8 | loop fusion | flops 6815744 | bytes 11534340 | tf_op jit(solution)/shard_map/convert_element_type | solution.py:31
Async XLA Ops:
  1.9 237.2 %copy-start = (f32[1,2048,256]{2,1,0:T(8,128)S(1)}, f32[1,2048,256]{2,1,0:T(8,128)}, u32[]{:S(2)}) copy-start(f32[1,2048,256]{2,1,0:T(8,128)} %param.15) | copy-start | bytes 6291460
  1.9 237.2 %copy-start.1 = (f32[1,2048,256]{2,1,0:T(8,128)S(1)}, f32[1,2048,256]{2,1,0:T(8,128)}, u32[]{:S(2)}) copy-start(f32[1,2048,256]{2,1,0:T(8,128)} %param.14) | copy-start | bytes 6291460
  239.1 5.1 %copy-start.2 = (f32[1,256,2048]{2,1,0:T(8,128)S(1)}, f32[1,256,2048]{2,1,0:T(8,128)}, u32[]{:S(2)}) copy-start(f32[1,256,2048]{2,1,0:T(8,128)} %param.17) | copy-start | bytes 6291460
  239.2 5.1 %copy-start.3 = (f32[1,256,2048]{2,1,0:T(8,128)S(1)}, f32[1,256,2048]{2,1,0:T(8,128)}, u32[]{:S(2)}) copy-start(f32[1,256,2048]{2,1,0:T(8,128)} %param.16) | copy-start | bytes 6291460
  239.2 5.0 %copy-start.4 = (f32[256,2048]{1,0:T(8,128)S(1)}, f32[256,2048]{1,0:T(8,128)}, u32[]{:S(2)}) copy-start(f32[256,2048]{1,0:T(8,128)} %get-tuple-element.11) | copy-start | bytes 6291460

commit v2 on v1

--- a/solution.py
+++ b/solution.py
@@ -69,6 +69,7 @@
     target = route * cap + within.astype(jnp.int32) - 1
     pl.semaphore_wait(barrier, experts + widths - 2)
 
+    depth = 3
     half_way = experts // 2
     order = [0] + sorted(range(1, experts), key=lambda d: (abs(d - half_way), d))
 
@@ -101,7 +102,8 @@
 
             if j:
                 g_copy(n, order[j]).start()
-                z_copy(n, order[j]).start()
+                if n < halves + depth:
+                    z_copy(n, order[j]).start()
 
     ge_ref[...] = jnp.zeros_like(ge_ref)
     gd_ref[...] = jnp.zeros_like(gd_ref)
@@ -136,6 +138,15 @@
         def _():
             z_copy(n, 1).wait_recv()
             g_copy(n, 1).wait_recv()
+            z_copy(n, 1).wait_send()
+
+        for j in range(1, experts):
+            later = n + depth
+            begin = max(j * halves, halves + depth)
+
+            @pl.when((n >= halves) & (later >= begin) & (later < (j + 1) * halves))
+            def _(j=j, later=later):
+                z_copy(later, order[j]).start()
 
         pre[n] = dot(rows[n], we_ref[...])
         for w in peers:
@@ -233,7 +244,6 @@
 
     @pl.loop(halves, count)
     def _(n):
-        z_copy(n, 1).wait_send()
         g_copy(n, 1).wait_send()
 
     @pl.loop(0, count)

time: 248 us -> 236 us (0.952)
  Pallas kernels: 235 us -> 223 us
    pallas_call x1, Pallas kernels: 235 us -> 223 us  [body(): pl.pallas_call(functools.partial(kernel, experts, widths, cap, chunk, til...]
where the time goes in v2:
time: 236 us
  Pallas kernels  223 us (94%)
  other arithmetic  8.31 us (4%)
  local copies, waits for them, and re-layouts  2.51 us (1%)
    pallas_call x1, Pallas kernels, body(): pl.pallas_call(functools.partial(kernel, experts, widths, cap, chunk, til...  223 us
    convert_element_type x2, other arithmetic, adam_step(): return (new_first, new_second, (corrected / (spread + ADAM_EPS)).astype(BF))  8.31 us

profile of v2, /device:TPU:0, one launch (start us, length us, event | category | flops | bytes accessed | tf_op | source)
XLA Modules:
  0.0 235.6 jit_solution(6735009542890643193)
XLA Ops:
  0.6 1.3 broadcast_in_dim.2.gate_ref
  1.9 0.0 copy-start
  1.9 0.0 copy-start.1
  1.9 223.4 %shard_map.136 = (f32[2048,256]{1,0:T(8,128)}, f32[256,2048]{1,0:T(8,128)}, f32[8,128]{1,0:T(8,128)}) custom-call(bf16[1024,2048]{1,0:T(8,128)(2,1)} %x_ref.1, s32[1,1024]{1,0:T(1,128)} %bitcast.22, bf16[16,1024]{1,0:T(8,128)(2,1)} %broadcast_in_dim.2.gate_ref, bf16[2048,256]{1,0:T(8,128)(2,1)} %bitcast.20, bf16[256,2048]{1,0:T(8,128)(2,1)} %bitcast.21), custom_call_target="tpu_custom_call" | custom-call | flops 10737418240 | bytes 8388608 | tf_op jit(solution)/shard_map/pallas_call | solution.py:276
  225.3 1.2 slice.3
  227.2 0.0 copy-done
  227.2 0.0 copy-done.1
  227.3 0.0 copy-start.2
  227.3 0.0 copy-start.3
  227.3 0.0 copy-start.4
  227.3 5.0 %divide_convert_fusion.1 = (bf16[1,2048,256]{2,1,0:T(8,128)(2,1)}, f32[1,2048,256]{2,1,0:T(8,128)}, f32[1,2048,256]{2,1,0:T(8,128)}) fusion(f32[2048,256]{1,0:T(8,128)} %get-tuple-element.10, f32[]{:T(128)} %bitcast.3, f32[1,2048,256]{2,1,0:T(8,128)S(1)} %copy-done, f32[1,2048,256]{2,1,0:T(8,128)S(1)} %copy-done.1), kind=kLoop, calls=%fused_computation.9 | loop fusion | flops 6815744 | bytes 11534340 | tf_op jit(solution)/shard_map/convert_element_type | solution.py:31
  232.3 0.0 copy-done.2
  232.3 0.0 copy-done.3
  232.3 0.0 copy-done.4
  232.3 3.3 %divide_convert_fusion = (bf16[1,256,2048]{2,1,0:T(8,128)(2,1)}, f32[1,256,2048]{2,1,0:T(8,128)}, f32[1,256,2048]{2,1,0:T(8,128)}) fusion(f32[256,2048]{1,0:T(8,128)S(1)} %copy-done.4, f32[]{:T(128)} %bitcast.3, f32[1,256,2048]{2,1,0:T(8,128)S(1)} %copy-done.2, f32[1,256,2048]{2,1,0:T(8,128)S(1)} %copy-done.3), kind=kLoop, calls=%fused_computation.8 | loop fusion | flops 6815744 | bytes 11534340 | tf_op jit(solution)/shard_map/convert_element_type | solution.py:31
Async XLA Ops:
  1.9 225.3 %copy-start = (f32[1,2048,256]{2,1,0:T(8,128)S(1)}, f32[1,2048,256]{2,1,0:T(8,128)}, u32[]{:S(2)}) copy-start(f32[1,2048,256]{2,1,0:T(8,128)} %param.15) | copy-start | bytes 6291460
  1.9 225.3 %copy-start.1 = (f32[1,2048,256]{2,1,0:T(8,128)S(1)}, f32[1,2048,256]{2,1,0:T(8,128)}, u32[]{:S(2)}) copy-start(f32[1,2048,256]{2,1,0:T(8,128)} %param.14) | copy-start | bytes 6291460
  227.3 5.1 %copy-start.2 = (f32[1,256,2048]{2,1,0:T(8,128)S(1)}, f32[1,256,2048]{2,1,0:T(8,128)}, u32[]{:S(2)}) copy-start(f32[1,256,2048]{2,1,0:T(8,128)} %param.17) | copy-start | bytes 6291460
  227.3 5.1 %copy-start.3 = (f32[1,256,2048]{2,1,0:T(8,128)S(1)}, f32[1,256,2048]{2,1,0:T(8,128)}, u32[]{:S(2)}) copy-start(f32[1,256,2048]{2,1,0:T(8,128)} %param.16) | copy-start | bytes 6291460
  227.3 5.0 %copy-start.4 = (f32[256,2048]{1,0:T(8,128)S(1)}, f32[256,2048]{1,0:T(8,128)}, u32[]{:S(2)}) copy-start(f32[256,2048]{1,0:T(8,128)} %get-tuple-element.11) | copy-start | bytes 6291460
